TPU v7x, 32 devices: a whole 2x2x4 slice. The times are simulated.
32 devices in a mesh: grp: 2 (over y), hid: 4 (over z), wid: 2 (over x), dat: 2 (over core).
Axes of the slice: x: 2, y: 2, z: 4, core: 2. Of those that a mesh axis runs over, the one named last changes fastest.
Arguments:
- tokens: bfloat16 [128, 4096], P(('grp', 'hid', 'dat'), 'wid'), parts along dimension 0, may hold values from -6 to 6
- output_gradient: bfloat16 [128, 4096], P(('grp', 'hid', 'dat'), 'wid'), parts along dimension 0, may hold values from -6 to 6
- gate_weight_blocks: bfloat16 [4, 2, 48, 128, 128], P('hid', 'wid'), may hold values from -0.125 to 0.125
- gate_block_places: int32 [4, 2, 48], P('hid', 'wid'), may hold values from 0 to 64, as said below
- up_weight_blocks: bfloat16 [4, 2, 48, 128, 128], P('hid', 'wid'), may hold values from -0.125 to 0.125
- up_block_places: int32 [4, 2, 48], P('hid', 'wid'), may hold values from 0 to 64, as said below
- down_weight_blocks: bfloat16 [4, 2, 48, 128, 128], P('hid', 'wid'), may hold values from -0.1875 to 0.1875
- down_block_places: int32 [4, 2, 48], P('hid', 'wid'), may hold values from 0 to 64, as said below
- gate_adapter_first: bfloat16 [4096, 16], P('wid'), may hold values from -0.09375 to 0.09375
- gate_adapter_second: bfloat16 [16, 2048], P(None, 'hid'), may hold values from -0.59765625 to 0.59765625
- up_adapter_first: bfloat16 [4096, 16], P('wid'), may hold values from -0.09375 to 0.09375
- up_adapter_second: bfloat16 [16, 2048], P(None, 'hid'), may hold values from -0.59765625 to 0.59765625
- down_adapter_first: bfloat16 [2048, 16], P('hid'), may hold values from -0.125 to 0.125
- down_adapter_second: bfloat16 [16, 4096], P(None, 'wid'), may hold values from -0.29882812 to 0.29882812
Outputs:
- token_gradient: bfloat16 [128, 4096], P(('grp', 'hid', 'dat'), 'wid'), parts along dimension 0
- gate_adapter_gradient: float32 [32, 2048], P('grp', 'hid'), parts along dimension 0
- up_adapter_gradient: float32 [32, 2048], P('grp', 'hid'), parts along dimension 0
- down_adapter_gradient: float32 [32, 4096], P('grp', 'wid'), parts along dimension 0
There are 2 independent parts, one for each index of `grp`. A program takes and returns all parts, laid end to end along the dimension named above; an argument that names none is the same for every part. Nothing has to cross between parts.
Inputs may be any that keep to these rules, and one draw needn't show every extreme that they name: `gate_block_places`: in each tile the live slots come first and name distinct block positions; the remaining slots hold 64. Some tile of the matrix has all 48 slots live. `up_block_places`: as for gate_block_places. `down_block_places`: as for gate_block_places.
All inputs are finite; a program needn't handle non-finite values.
Results may differ from a plain program's by a relative error of at most 0.0049.
Values may be sent and summed in bfloat16 or wider, within the bound.
A program may use at most 64 MiB of HBM per device.

v0:
```python
import jax
import jax.numpy as jnp
from jax import lax
from jax.sharding import PartitionSpec as P

adapter_scale = 2.0
highest_precision = lax.Precision.HIGHEST


def wide_dot(left, right):
    return jnp.dot(left.astype(jnp.float32), right.astype(jnp.float32), precision=highest_precision)


def into_hidden(row_block, tile_values, slot_index, hidden_block_count, wid_blocks, pattern):
    row_count = row_block.shape[0]
    block_step = tile_values.shape[-1]
    split_rows = row_block.reshape(row_count, wid_blocks, block_step)
    picked = jnp.take(split_rows, slot_index % wid_blocks, axis=1)
    product = jnp.einsum(pattern, picked, tile_values, preferred_element_type=jnp.float32)
    onehot = (slot_index[:, None] // wid_blocks == jnp.arange(hidden_block_count)[None, :]).astype(
        jnp.float32
    )
    merged = jnp.einsum("rkj,kh->rhj", product, onehot, precision=highest_precision)
    return merged.reshape(row_count, hidden_block_count * block_step)


def into_width(row_block, tile_values, slot_index, hidden_block_count, wid_blocks):
    row_count = row_block.shape[0]
    block_step = tile_values.shape[-1]
    split_rows = row_block.reshape(row_count, hidden_block_count, block_step)
    which_hidden = jnp.minimum(slot_index // wid_blocks, hidden_block_count - 1)
    picked = jnp.take(split_rows, which_hidden, axis=1)
    product = jnp.einsum("rkj,kcj->rkc", picked, tile_values, preferred_element_type=jnp.float32)
    live_slot = slot_index < hidden_block_count * wid_blocks
    onehot = (
        ((slot_index % wid_blocks)[:, None] == jnp.arange(wid_blocks)[None, :]) & live_slot[:, None]
    ).astype(jnp.float32)
    merged = jnp.einsum("rkc,kw->rwc", product, onehot, precision=highest_precision)
    return merged.reshape(row_count, wid_blocks * block_step)


def shards(
    tokens,
    output_gradient,
    gate_weight_blocks,
    gate_block_places,
    up_weight_blocks,
    up_block_places,
    down_weight_blocks,
    down_block_places,
    gate_adapter_first,
    gate_adapter_second,
    up_adapter_first,
    up_adapter_second,
    down_adapter_first,
    down_adapter_second,
):
    gate_vals, gate_index = (gate_weight_blocks[0, 0], gate_block_places[0, 0])
    up_vals, up_index = (up_weight_blocks[0, 0], up_block_places[0, 0])
    down_vals, down_index = (down_weight_blocks[0, 0], down_block_places[0, 0])
    block_step = gate_vals.shape[-1]
    hidden_block_count = gate_adapter_second.shape[1] // block_step
    wid_blocks = tokens.shape[1] // block_step
    token_row_slice, gradient_rows = (
        lax.all_gather(tokens, "hid", axis=0, tiled=True),
        lax.all_gather(output_gradient, "hid", axis=0, tiled=True),
    )
    gate_piece = into_hidden(
        token_row_slice, gate_vals, gate_index, hidden_block_count, wid_blocks, "rkc,kcj->rkj"
    )
    up_piece = into_hidden(
        token_row_slice, up_vals, up_index, hidden_block_count, wid_blocks, "rkc,kcj->rkj"
    )
    gate_rank_rows = wide_dot(token_row_slice, gate_adapter_first)
    up_rank_rows = wide_dot(token_row_slice, up_adapter_first)
    down_piece = into_hidden(
        gradient_rows, down_vals, down_index, hidden_block_count, wid_blocks, "rkc,kjc->rkj"
    )
    rank_gradient = wide_dot(gradient_rows, down_adapter_second.T)
    gate_piece, up_piece, down_piece, gate_rank_rows, up_rank_rows, rank_gradient = lax.psum(
        (gate_piece, up_piece, down_piece, gate_rank_rows, up_rank_rows, rank_gradient), "wid"
    )
    gate_activation = gate_piece + adapter_scale * wide_dot(gate_rank_rows, gate_adapter_second)
    up_activation = up_piece + adapter_scale * wide_dot(up_rank_rows, up_adapter_second)
    hidden_gradient = down_piece + adapter_scale * wide_dot(rank_gradient, down_adapter_first.T)
    sigmoid_gate = jax.nn.sigmoid(gate_activation)
    activated = gate_activation * sigmoid_gate
    hidden_state = (activated * up_activation).astype(jnp.bfloat16)
    gate_gradient = (
        hidden_gradient
        * up_activation
        * sigmoid_gate
        * (1.0 + gate_activation * (1.0 - sigmoid_gate))
    ).astype(jnp.bfloat16)
    up_gradient = (hidden_gradient * activated).astype(jnp.bfloat16)
    gate_backward = wide_dot(gate_gradient, gate_adapter_second.T)
    up_backward = wide_dot(up_gradient, up_adapter_second.T)
    down_rank_piece = wide_dot(hidden_state, down_adapter_first)
    gate_adapter_widened = gate_adapter_first.T.astype(jnp.float32)
    up_adapter_widened = up_adapter_first.T.astype(jnp.float32)
    term_value = into_width(gate_gradient, gate_vals, gate_index, hidden_block_count, wid_blocks)
    term_value = term_value + into_width(
        up_gradient, up_vals, up_index, hidden_block_count, wid_blocks
    )
    rank_product = jnp.dot(
        gate_backward, gate_adapter_widened, precision=highest_precision
    ) + jnp.dot(up_backward, up_adapter_widened, precision=highest_precision)
    token_gradient = lax.psum_scatter(
        term_value + adapter_scale * rank_product, "hid", scatter_dimension=0, tiled=True
    ).astype(jnp.bfloat16)
    gate_gradient_piece = adapter_scale * jnp.dot(
        gate_rank_rows.T, gate_gradient.astype(jnp.float32), precision=highest_precision
    )
    up_gradient_piece = adapter_scale * jnp.dot(
        up_rank_rows.T, up_gradient.astype(jnp.float32), precision=highest_precision
    )
    width_gradient = gradient_rows.astype(jnp.float32)
    down_rank_rows = lax.psum(down_rank_piece, "hid")
    down_gradient_piece = adapter_scale * jnp.dot(
        down_rank_rows.T, width_gradient, precision=highest_precision
    )
    gate_adapter_gradient, up_adapter_gradient, down_adapter_gradient = lax.psum(
        (gate_gradient_piece, up_gradient_piece, down_gradient_piece), "dat"
    )
    return (token_gradient, gate_adapter_gradient, up_adapter_gradient, down_adapter_gradient)


def solution(mesh):
    return jax.shard_map(
        shards,
        mesh=mesh,
        in_specs=(
            P(("grp", "hid", "dat"), "wid"),
            P(("grp", "hid", "dat"), "wid"),
            P("hid", "wid", None, None, None),
            P("hid", "wid", None),
            P("hid", "wid", None, None, None),
            P("hid", "wid", None),
            P("hid", "wid", None, None, None),
            P("hid", "wid", None),
            P("wid", None),
            P(None, "hid"),
            P("wid", None),
            P(None, "hid"),
            P("hid", None),
            P(None, "wid"),
        ),
        out_specs=(
            P(("grp", "hid", "dat"), "wid"),
            P("grp", "hid"),
            P("grp", "hid"),
            P("grp", "wid"),
        ),
        check_vma=False,
    )
```

profile of v0, /device:TPU:0, one launch (start us, length us, event | category | flops | bytes accessed | tf_op | source)
XLA Modules:
  0.0 164.7 jit_solution(8176587963584873713)
XLA Ops:
  7.2 0.0 copy-start
  7.2 0.0 all-reduce.11.cloned.1.call-start
  7.2 0.8 compare_and_fusion.4
  8.0 0.7 and_select_fusion.4
  8.7 1.3 compare_and_fusion
  10.0 0.6 copy-done.22
  10.5 15.3 %all_gather.7 = bf16[32,2048]{1,0:T(8,128)(2,1)S(1)} all-gather(bf16[8,2048]{1,0:T(8,128)(2,1)} %param.18), channel_id=1, replica_groups=mesh['grp'=2,'hid'=4,'wid'=2,'dat'=2] {'hid'}, dimensions={0}, use_global_device_ids=true | all-gather | bytes 163840 | tf_op jit(solution)/shard_map/all_gather | solution.py:65
  25.8 1.2 compare_and_fusion.1
  27.0 0.5 copy-done.19
  27.6 1.4 gather_fusion.1
  28.9 1.4 gather_fusion.2
  30.3 13.5 %all_gather.6 = bf16[32,2048]{1,0:T(8,128)(2,1)S(1)} all-gather(bf16[8,2048]{1,0:T(8,128)(2,1)S(1)} %copy-done.13), channel_id=1, replica_groups=mesh['grp'=2,'hid'=4,'wid'=2,'dat'=2] {'hid'}, dimensions={0}, use_global_device_ids=true | all-gather | bytes 163840 | tf_op jit(solution)/shard_map/all_gather | solution.py:66
  43.9 1.4 gather_fusion
  45.2 2.6 %fusion.12 = f32[32,48,128]{2,0,1:T(8,128)S(1)} fusion(bf16[1,1,48,128,128]{4,3,2,1,0:T(8,128)(2,1)} %param.24, bf16[48,32,128]{2,1,0:T(8,128)(2,1)} %gather_fusion, pred[48]{0:T(512)(128)(4,1)S(1)} %get-tuple-element.22), kind=kOutput, calls=%fused_computation.19 | convolution fusion | flops 50528256 | bytes 2752560 | tf_op jit(solution)/shard_map/rkc,kjc->rkj/dot_general | solution.py:19
  47.8 0.8 fusion.37
  48.7 0.6 copy.56
  49.3 0.6 fusion.15
  49.9 0.8 fusion.35
  50.7 0.0 copy-start.25
  50.8 0.6 fusion.21
  51.3 0.0 copy-done.25
  51.4 0.8 fusion.33
  52.2 0.7 copy_bitcast_fusion.2
  52.8 0.0 all-reduce.11.cloned.1.call-update
  52.8 0.0 reduce-scatter.2.cloned.1.call-start
  52.9 1.6 fusion.87
  54.5 0.8 fusion.88
  55.3 0.8 fusion.89
  56.0 9.5 %all-reduce.1 = (f32[32,16]{0,1:T(8,128)S(1)}, f32[32,16]{0,1:T(8,128)}, f32[32,16]{0,1:T(8,128)S(1)}) all-reduce(f32[32,16]{0,1:T(8,128)} %fusion.89, f32[32,16]{0,1:T(8,128)} %fusion.87, f32[32,16]{0,1:T(8,128)} %fusion.88), channel_id=1, replica_groups=mesh['grp'=2,'hid'=4,'wid'=2,'dat'=2] {'wid'}, use_global_device_ids=true, to_apply=%region_5.7 | all-reduce | flops 1536 | bytes 12288 | tf_op jit(solution)/shard_map/psum | solution.py:80
  65.6 1.2 pad_clamp_fusion.1
  66.8 1.3 pad_clamp_fusion
  68.0 8.9 %all-reduce.11.cloned.1.call-done = (f32[32,512]{1,0:T(8,128)}, f32[32,512]{1,0:T(8,128)}, f32[32,512]{1,0:T(8,128)}) async-done(((f32[32,512]{1,0:T(8,128)}, f32[32,512]{1,0:T(8,128)}, f32[32,512]{1,0:T(8,128)}), (f32[32,512]{1,0:T(8,128)}, f32[32,512]{1,0:T(8,128)}, f32[32,512]{1,0:T(8,128)})) %all-reduce.11.cloned.1.call-update) | async-done | bytes 196624 | tf_op jit(solution)/shard_map/psum | solution.py:80
  77.0 1.1 fusion.28
  78.1 1.1 fusion.27
  79.2 1.1 multiply_convert_fusion.1
  80.4 0.1 fusion.90
  80.5 0.8 fusion.92
  81.3 1.0 fusion.91
  82.3 1.5 gather_fusion.3
  83.8 2.0 %fusion.24 = f32[32,48,128]{2,0,1:T(8,128)S(1)} fusion(bf16[1,1,48,128,128]{4,3,2,1,0:T(8,128)(2,1)S(1)} %copy-done, bf16[48,32,128]{2,1,0:T(8,128)(2,1)} %gather_fusion.3, pred[48]{0:T(512)(128)(4,1)} %get-tuple-element.17), kind=kOutput, calls=%fused_computation.23 | convolution fusion | flops 50528256 | bytes 2752560 | tf_op jit(solution)/shard_map/rkj,kcj->rkc/dot_general | solution.py:33
  85.8 0.0 copy-done.18
  85.8 1.5 fusion.31
  87.3 1.5 gather_fusion.4
  88.8 2.0 %fusion.18 = f32[32,48,128]{2,0,1:T(8,128)S(1)} fusion(bf16[1,1,48,128,128]{4,3,2,1,0:T(8,128)(2,1)S(1)} %copy-done.1, bf16[48,32,128]{2,1,0:T(8,128)(2,1)} %gather_fusion.4, pred[48]{0:T(512)(128)(4,1)S(1)} %copy-done.24), kind=kOutput, calls=%fused_computation.21 | convolution fusion | flops 50528256 | bytes 2752560 | tf_op jit(solution)/shard_map/rkj,kcj->rkc/dot_general | solution.py:33
  90.9 0.0 copy-start.26
  90.9 0.8 convolution_add_fusion.1
  91.8 1.1 fusion.1
  92.8 0.0 reduce-scatter.2.cloned.1.call-update
  92.9 0.0 all-reduce.9.cloned.1.call-start
  93.0 0.1 fusion.60
  93.1 12.2 %psum.78 = f32[32,16]{0,1:T(8,128)S(1)} all-reduce(f32[32,16]{0,1:T(8,128)S(1)} %fusion.60), channel_id=1, replica_groups=mesh['grp'=2,'hid'=4,'wid'=2,'dat'=2] {'hid'}, use_global_device_ids=true, to_apply=%region_9.12 | all-reduce | flops 512 | bytes 4096 | tf_op jit(solution)/shard_map/psum | solution.py:118
  105.3 0.8 convolution_multiply_fusion.4
  106.1 0.8 convolution_multiply_fusion.5
  106.8 0.0 all-reduce.9.cloned.1.call-update
  106.9 0.0 all-reduce.7.cloned.1.call-start
  106.9 0.9 convolution_multiply_fusion
  107.8 0.0 all-reduce.7.cloned.1.call-update
  107.8 4.8 %reduce-scatter.2.cloned.1.call-done = f32[8,2048]{1,0:T(8,128)} async-done(((f32[32,2048]{1,0:T(8,128)}), f32[8,2048]{1,0:T(8,128)}) %reduce-scatter.2.cloned.1.call-update) | async-done | bytes 65552 | tf_op jit(solution)/shard_map/reduce_scatter | solution.py:108
  112.6 1.5 convert_element_type.10
  114.0 17.8 %all-reduce.9.cloned.1.call-done = (f32[16,512]{1,0:T(8,128)}, f32[16,512]{1,0:T(8,128)}) async-done(((f32[16,512]{1,0:T(8,128)}, f32[16,512]{1,0:T(8,128)}), (f32[16,512]{1,0:T(8,128)}, f32[16,512]{1,0:T(8,128)})) %all-reduce.9.cloned.1.call-update) | async-done | bytes 65552 | tf_op jit(solution)/shard_map/psum | solution.py:122
  131.8 22.0 %all-reduce.7.cloned.1.call-done = f32[16,2048]{1,0:T(8,128)} async-done(((f32[16,2048]{1,0:T(8,128)}), f32[16,2048]{1,0:T(8,128)}) %all-reduce.7.cloned.1.call-update) | async-done | bytes 131088 | tf_op jit(solution)/shard_map/psum | solution.py:122
  153.8 1.4 copy.63
  155.2 1.4 copy.64
  156.6 1.6 copy.65
  (56 shorter events, 0.2 us)
Async XLA Ops:
  7.2 43.5 %copy-start = (bf16[1,1,48,128,128]{4,3,2,1,0:T(8,128)(2,1)S(1)}, bf16[1,1,48,128,128]{4,3,2,1,0:T(8,128)(2,1)}, u32[]{:S(2)}) copy-start(bf16[1,1,48,128,128]{4,3,2,1,0:T(8,128)(2,1)} %param.20) | copy-start | bytes 4718596
  7.2 23.1 %copy-start.13 = (bf16[8,2048]{1,0:T(8,128)(2,1)S(1)}, bf16[8,2048]{1,0:T(8,128)(2,1)}, u32[]{:S(2)}) copy-start(bf16[8,2048]{1,0:T(8,128)(2,1)} %param.19) | copy-start | bytes 98308
  7.2 69.8 %all-reduce.11.cloned.1.call-start = ((), (), s32[]{:S(2)}) async-start(), calls=%async_computation.4 | async-start | bytes 393216 | tf_op jit(solution)/shard_map/psum | solution.py:80
  9.9 0.6 copy-start.22
  27.0 0.5 copy-start.19
  45.2 4.1 %copy-start.1 = (bf16[1,1,48,128,128]{4,3,2,1,0:T(8,128)(2,1)S(1)}, bf16[1,1,48,128,128]{4,3,2,1,0:T(8,128)(2,1)}, u32[]{:S(2)}) copy-start(bf16[1,1,48,128,128]{4,3,2,1,0:T(8,128)(2,1)} %param.22) | copy-start | bytes 4718596
  45.2 4.1 %copy-start.3 = (bf16[48,32,128]{2,1,0:T(8,128)(2,1)S(1)}, bf16[48,32,128]{2,1,0:T(8,128)(2,1)}, u32[]{:S(2)}) copy-start(bf16[48,32,128]{2,1,0:T(8,128)(2,1)} %gather_fusion.1) | copy-start | bytes 1179652
  49.3 1.4 copy-start.2
  50.7 0.7 copy-start.25
  50.7 3.8 %copy-start.7 = (bf16[2048,16]{0,1:T(8,128)(2,1)S(1)}, bf16[2048,16]{0,1:T(8,128)(2,1)}, u32[]{:S(2)}) copy-start(bf16[2048,16]{0,1:T(8,128)(2,1)} %param.28) | copy-start | bytes 196612
  50.7 4.5 %copy-start.6 = (bf16[2048,16]{0,1:T(8,128)(2,1)S(1)}, bf16[2048,16]{0,1:T(8,128)(2,1)}, u32[]{:S(2)}) copy-start(bf16[2048,16]{0,1:T(8,128)(2,1)} %param.26) | copy-start | bytes 196612
  51.3 26.7 %copy-start.8 = (bf16[16,512]{1,0:T(8,128)(2,1)S(1)}, bf16[16,512]{1,0:T(8,128)(2,1)}, u32[]{:S(2)}) copy-start(bf16[16,512]{1,0:T(8,128)(2,1)} %param.27) | copy-start | bytes 49156
  52.8 59.7 %reduce-scatter.2.cloned.1.call-start = ((), (), s32[]{:S(2)}) async-start(), calls=%async_computation.1 | async-start | bytes 327680 | tf_op jit(solution)/shard_map/reduce_scatter | solution.py:108
  65.6 13.6 %copy-start.14 = (f32[32,16]{0,1:T(8,128)}, f32[32,16]{0,1:T(8,128)S(1)}, u32[]{:S(2)}) copy-start(f32[32,16]{0,1:T(8,128)S(1)} %get-tuple-element.8) | copy-start | bytes 6148
  65.6 13.6 %copy-start.16 = (f32[32,16]{0,1:T(8,128)}, f32[32,16]{0,1:T(8,128)S(1)}, u32[]{:S(2)}) copy-start(f32[32,16]{0,1:T(8,128)S(1)} %get-tuple-element.10) | copy-start | bytes 6148
  78.1 2.3 %copy-start.9 = (f32[32,512]{1,0:T(8,128)}, f32[32,512]{1,0:T(8,128)S(1)}, u32[]{:S(2)}) copy-start(f32[32,512]{1,0:T(8,128)S(1)} %fusion.28) | copy-start | bytes 196612
  79.2 1.3 copy-start.11
  83.8 2.0 %copy-start.18 = (pred[48]{0:T(512)(128)(4,1)S(1)}, pred[48]{0:T(512)(128)(4,1)}, u32[]{:S(2)}) copy-start(pred[48]{0:T(512)(128)(4,1)} %get-tuple-element.29) | copy-start | bytes 148
  83.8 2.0 %copy-start.20 = (s32[48]{0:T(128)S(1)}, s32[48]{0:T(128)}, u32[]{:S(2)}) copy-start(s32[48]{0:T(128)} %copy-done.19) | copy-start | bytes 580
  85.8 3.1 %copy-start.24 = (pred[48]{0:T(512)(128)(4,1)S(1)}, pred[48]{0:T(512)(128)(4,1)}, u32[]{:S(2)}) copy-start(pred[48]{0:T(512)(128)(4,1)} %get-tuple-element.14) | copy-start | bytes 148
  88.8 2.1 %copy-start.5 = (f32[16,32,128]{2,0,1:T(8,128)S(1)}, f32[16,32,128]{2,0,1:T(8,128)}, u32[]{:S(2)}) copy-start(f32[16,32,128]{2,0,1:T(8,128)} %fusion.31) | copy-start | bytes 786436
  88.8 2.1 %copy-start.21 = (pred[48]{0:T(512)(128)(4,1)S(1)}, pred[48]{0:T(512)(128)(4,1)}, u32[]{:S(2)}) copy-start(pred[48]{0:T(512)(128)(4,1)} %get-tuple-element.28) | copy-start | bytes 148
  88.8 2.1 %copy-start.23 = (s32[48]{0:T(128)S(1)}, s32[48]{0:T(128)}, u32[]{:S(2)}) copy-start(s32[48]{0:T(128)} %copy-done.22) | copy-start | bytes 580
  88.8 2.9 %copy-start.4 = (f32[32,2048]{1,0:T(8,128)S(1)}, f32[32,2048]{1,0:T(8,128)}, u32[]{:S(2)}) copy-start(f32[32,2048]{1,0:T(8,128)} %fusion.91) | copy-start | bytes 786436
  90.9 2.1 %copy-start.10 = (f32[32,512]{1,0:T(8,128)S(1)}, f32[32,512]{1,0:T(8,128)}, u32[]{:S(2)}) copy-start(f32[32,512]{1,0:T(8,128)} %copy-done.9) | copy-start | bytes 196612
  90.9 2.1 %copy-start.12 = (f32[32,512]{1,0:T(8,128)S(1)}, f32[32,512]{1,0:T(8,128)}, u32[]{:S(2)}) copy-start(f32[32,512]{1,0:T(8,128)} %copy-done.11) | copy-start | bytes 196612
  90.9 2.1 %copy-start.26 = (bf16[512,16]{0,1:T(8,128)(2,1)S(1)}, bf16[512,16]{0,1:T(8,128)(2,1)}, u32[]{:S(2)}) copy-start(bf16[512,16]{0,1:T(8,128)(2,1)} %param.30) | copy-start | bytes 49156
  90.9 14.4 %copy-start.17 = (f32[32,16]{0,1:T(8,128)S(1)}, f32[32,16]{0,1:T(8,128)}, u32[]{:S(2)}) copy-start(f32[32,16]{0,1:T(8,128)} %copy-done.16) | copy-start | bytes 6148
  90.9 15.2 %copy-start.15 = (f32[32,16]{0,1:T(8,128)S(1)}, f32[32,16]{0,1:T(8,128)}, u32[]{:S(2)}) copy-start(f32[32,16]{0,1:T(8,128)} %copy-done.14) | copy-start | bytes 6148
  92.9 39.0 %all-reduce.9.cloned.1.call-start = ((), (), s32[]{:S(2)}) async-start(), calls=%async_computation.3 | async-start | bytes 131072 | tf_op jit(solution)/shard_map/psum | solution.py:122
  106.9 46.9 %all-reduce.7.cloned.1.call-start = ((), (), s32[]{:S(2)}) async-start(), calls=%async_computation.2 | async-start | bytes 262144 | tf_op jit(solution)/shard_map/psum | solution.py:122
Sparse Core Ops, SparseCore 0:
  53.0 23.9 all-reduce.10
  93.0 19.5 reduce-scatter.1
  115.6 16.1 all-reduce.8
  134.7 19.0 all-reduce.6
where the time goes:
time: 166 us; the launch traced here: 165 us
  waiting for transfers between devices  53.5 us (32%)
  blocking collectives  50.5 us (30%)
  matrix products  24.5 us (15%)
  between operations  14.1 us (8%)
  local copies, waits for them, and re-layouts  14 us (8%)
  other arithmetic  7.89 us (5%)
    psum x2, waiting for transfers between devices, shards(): lax.psum((gate_gradient_piece, up_gradient_piece, down_gradient_piece), '...  39.8 us
    all_gather x1, blocking collectives, shards(): lax.all_gather(tokens, 'hid', axis=0, tiled=True)  15.3 us
    all_gather x1, blocking collectives, shards(): lax.all_gather(output_gradient, 'hid', axis=0, tiled=True)  13.5 us
    psum x1, blocking collectives, shards(): down_rank_rows = lax.psum(down_rank_piece, 'hid')  12.2 us
    psum x1, blocking collectives, shards(): lax.psum((gate_piece, up_piece, down_piece, gate_rank_rows, up_rank_rows,...  9.54 us
    psum x1, waiting for transfers between devices, shards(): lax.psum((gate_piece, up_piece, down_piece, gate_rank_rows, up_rank_rows,...  8.93 us
    dot_general x9, matrix products, wide_dot(): jnp.dot(left.astype(jnp.float32), right.astype(jnp.float32), precision=hi...  7.49 us
    unnamed x58, local copies, waits for them, and re-layouts  6.18 us
  transfers between devices with their start and end apart: 4, of which 4 were waited for; matrix products, arithmetic and copies ran while one was open for 6% of the time, Pallas kernels for 0%

commit v1 on v0

v1 whole, which is shorter than its diff:
```python
import functools

import jax
import jax.numpy as jnp
from jax import lax
from jax.experimental import pallas as pl
from jax.experimental.pallas import tpu as pltpu
from jax.sharding import PartitionSpec as P

adapter_scale = 2.0
MESH = pl.DeviceIdType.MESH
bf16, f32 = jnp.bfloat16, jnp.float32


def dot(left, right):
    return jnp.dot(left, right, preferred_element_type=f32)


def dot_nt(left, right):
    return lax.dot_general(left, right, (((1,), (1,)), ((), ())), preferred_element_type=f32)


def two_parts(value):
    high = value.astype(bf16)
    low = (value - high.astype(f32)).astype(bf16)
    return jnp.concatenate([high, low], axis=0)


def wide(product):
    half = product.shape[0] // 2
    return product[:half] + product[half:]


def kernel(
    n_hid, n_wid, n_dat,
    tok, dy, wg, wu, wd, pg, pu, pd, ag, bg, au, bu, ad, bd,
    tok_out, gate_out, up_out, down_out,
    slots, inv_v, inv_s, wcat, wdn, bcat, a_first, a2, ad_v, bd_v,
    xg, yg, x_v, y_v, fbuf, rbuf, hbuf, sbuf, tbuf, dbuf, gbuf, ebuf, acc,
    local_sem, x_s, x_r, y_s, y_r, f_s, f_r, r_s, r_r, h_s, h_r, t_s, t_r, d_s, d_r, g_s, g_r, e_s, e_r,
):
    me_h, me_w, me_d = lax.axis_index("hid"), lax.axis_index("wid"), lax.axis_index("dat")
    own, width = tok.shape
    rows = own * n_hid
    cap, step = wg.shape[2], wg.shape[3]
    hid = bg.shape[1]
    rank = bg.shape[0]
    hb, wb = hid // step, width // step

    def peers(me, n):
        return [lax.rem(me + d, n) for d in range(1, n)]

    groups = (("hid", me_h, n_hid), ("wid", me_w, n_wid), ("dat", me_d, n_dat))
    barrier = pltpu.get_barrier_semaphore()
    for axis, me, n in groups:
        for peer in peers(me, n):
            pl.semaphore_signal(barrier, inc=1, device_id={axis: peer}, device_id_type=MESH)

    pairs = [
        (tok, xg.at[me_h]),
        (dy, yg.at[me_h]),
        (wg.at[0, 0], slots.at[0, pl.ds(0, cap)]),
        (wu.at[0, 0], slots.at[1, pl.ds(0, cap)]),
        (wd.at[0, 0], slots.at[2, pl.ds(0, cap)]),
        (ag, a_first.at[0]),
        (au, a_first.at[1]),
        (bg, bcat.at[pl.ds(0, rank), pl.ds(0, hid)]),
        (bu, bcat.at[pl.ds(rank, rank), pl.ds(hid, hid)]),
        (ad, ad_v),
        (bd, bd_v),
    ]
    local = [pltpu.make_async_copy(s, d, local_sem.at[i]) for i, (s, d) in enumerate(pairs)]
    for copy in local:
        copy.start()

    pl.semaphore_wait(barrier, n_hid + n_wid + n_dat - 3)

    def send(source, buf, axis, me, n, send_sem, recv_sem):
        copies = []
        for d, peer in enumerate(peers(me, n)):
            copy = pltpu.make_async_remote_copy(
                src_ref=source(peer), dst_ref=buf.at[me],
                send_sem=send_sem.at[d], recv_sem=recv_sem.at[me],
                device_id={axis: peer}, device_id_type=MESH,
            )
            copy.start()
            copies.append(copy)
        return copies

    def arrive(buf, axis, me, n, send_sem, recv_sem):
        for d, peer in enumerate(peers(me, n)):
            pltpu.make_async_remote_copy(
                src_ref=buf.at[peer], dst_ref=buf.at[peer],
                send_sem=send_sem.at[d], recv_sem=recv_sem.at[peer],
                device_id={axis: peer}, device_id_type=MESH,
            ).wait_recv()

    hid_axis, wid_axis, dat_axis = groups
    sent = send(lambda peer: tok, xg, *hid_axis, x_s, x_r)
    sent += send(lambda peer: dy, yg, *hid_axis, y_s, y_r)

    lanes = inv_v.shape[1]
    lane = lax.broadcasted_iota(jnp.int32, (8, lanes), 1)
    row = lax.broadcasted_iota(jnp.int32, (8, lanes), 0)
    inverse = jnp.full((8, lanes), cap, jnp.int32)
    for m, places in enumerate((pg, pu, pd)):
        mine = jnp.where(row == m, lane, -1)
        for k in range(cap):
            inverse = jnp.where(mine == places[0, 0, k], k, inverse)
    inv_v[...] = inverse
    inv_copy = pltpu.make_async_copy(inv_v, inv_s, local_sem.at[len(pairs)])
    inv_copy.start()
    for m in range(3):
        slots[m, cap] = jnp.zeros((step, step), bf16)
    bcat[:rank, hid:] = jnp.zeros((rank, hid), bf16)
    bcat[rank:, :hid] = jnp.zeros((rank, hid), bf16)
    for copy in local[5:]:
        copy.wait()
    a2[:, :rank] = a_first[0]
    a2[:, rank:] = a_first[1]
    inv_copy.wait()
    for copy in local[2:5]:
        copy.wait()

    def lay(w, carry):
        start = pl.multiple_of(w * step, step)
        for h in range(hb):
            for m in range(2):
                wcat[pl.ds(start, step), m * hid + h * step : m * hid + (h + 1) * step] = slots[
                    m, inv_s[m, h * wb + w]
                ]
            wdn[h * step : (h + 1) * step, pl.ds(start, step)] = slots[2, inv_s[2, h * wb + w]]
        return carry

    lax.fori_loop(0, wb, lay, 0)

    def assemble(gathered, whole):
        parts = [gathered[i].astype(f32) for i in range(n_hid)]
        whole[...] = jnp.concatenate(parts, axis=0).astype(bf16)

    local[0].wait()
    arrive(xg, *hid_axis, x_s, x_r)
    assemble(xg, x_v)
    ranks = dot(x_v[...], a2[...])
    rbuf[me_w] = ranks
    low_rank = wide(dot(two_parts(ranks), bcat[...]))
    fbuf[me_w] = (dot(x_v[...], wcat[...]) + adapter_scale * low_rank).astype(bf16)
    sent += send(lambda peer: fbuf.at[me_w], fbuf, *wid_axis, f_s, f_r)
    sent += send(lambda peer: rbuf.at[me_w], rbuf, *wid_axis, r_s, r_r)

    local[1].wait()
    arrive(yg, *hid_axis, y_s, y_r)
    assemble(yg, y_v)
    grad_rank = dot_nt(y_v[...], bd_v[...])
    back_low = wide(dot_nt(two_parts(grad_rank), ad_v[...]))
    hbuf[me_w] = (dot_nt(y_v[...], wdn[...]) + adapter_scale * back_low).astype(bf16)
    sent += send(lambda peer: hbuf.at[me_w], hbuf, *wid_axis, h_s, h_r)

    arrive(fbuf, *wid_axis, f_s, f_r)
    arrive(rbuf, *wid_axis, r_s, r_r)
    both = sum(fbuf[i].astype(f32) for i in range(n_wid))
    ranks = sum(rbuf[i] for i in range(n_wid))
    gate, up = both[:, :hid], both[:, hid:]
    sig = jax.nn.sigmoid(gate)
    act = gate * sig
    hidden = (act * up).astype(bf16)
    dbuf[me_h] = dot(hidden, ad_v[...])
    sent += send(lambda peer: dbuf.at[me_h], dbuf, *hid_axis, d_s, d_r)
    slope = up * sig * (1.0 + gate * (1.0 - sig))
    arrive(hbuf, *wid_axis, h_s, h_r)
    hidden_grad = sum(hbuf[i].astype(f32) for i in range(n_wid))
    grads = jnp.concatenate(
        [(hidden_grad * slope).astype(bf16), (hidden_grad * act).astype(bf16)], axis=1
    )
    backs = two_parts(adapter_scale * dot_nt(grads, bcat[...]))
    total = dot_nt(grads, wcat[...]) + wide(dot_nt(backs, a2[...]))
    for i in range(n_hid):
        sbuf[i] = total[i * own : (i + 1) * own].astype(bf16)
    acc[...] = total.reshape(n_hid, own, width)
    sent += send(lambda peer: sbuf.at[peer], tbuf, *hid_axis, t_s, t_r)

    ranks_t = adapter_scale * ranks.T
    gbuf[me_d, :, :hid] = wide(dot(two_parts(ranks_t[:rank]), grads[:, :hid]))
    gbuf[me_d, :, hid:] = wide(dot(two_parts(ranks_t[rank:]), grads[:, hid:]))
    sent += send(lambda peer: gbuf.at[me_d], gbuf, *dat_axis, g_s, g_r)

    arrive(dbuf, *hid_axis, d_s, d_r)
    down_rank = adapter_scale * sum(dbuf[i] for i in range(n_hid)).T
    ebuf[me_d] = wide(dot(two_parts(down_rank), y_v[...]))
    sent += send(lambda peer: ebuf.at[me_d], ebuf, *dat_axis, e_s, e_r)

    arrive(gbuf, *dat_axis, g_s, g_r)
    summed = sum(gbuf[i] for i in range(n_dat))
    gate_out[...] = summed[:, :hid]
    up_out[...] = summed[:, hid:]
    arrive(tbuf, *hid_axis, t_s, t_r)
    mine = acc[me_h]
    for peer in peers(me_h, n_hid):
        mine = mine + tbuf[peer].astype(f32)
    tok_out[...] = mine.astype(bf16)
    arrive(ebuf, *dat_axis, e_s, e_r)
    down_out[...] = sum(ebuf[i] for i in range(n_dat))
    for copy in sent:
        copy.wait_send()


def shards(
    n_hid, n_wid, n_dat,
    tokens, output_gradient,
    gate_weight_blocks, gate_block_places,
    up_weight_blocks, up_block_places,
    down_weight_blocks, down_block_places,
    gate_adapter_first, gate_adapter_second,
    up_adapter_first, up_adapter_second,
    down_adapter_first, down_adapter_second,
):
    own, width = tokens.shape
    rows = own * n_hid
    cap, step = gate_weight_blocks.shape[2], gate_weight_blocks.shape[3]
    rank, hid = gate_adapter_second.shape
    positions = (hid // step) * (width // step)
    lanes = -(-positions // 128) * 128
    any_spec = pl.BlockSpec(memory_space=pl.ANY)
    smem_spec = pl.BlockSpec(memory_space=pltpu.SMEM)
    vmem_spec = pl.BlockSpec(memory_space=pltpu.VMEM)
    V = pltpu.VMEM
    D = pltpu.SemaphoreType.DMA

    def sems(n):
        return [D((max(n - 1, 1),)), D((n,))]

    return pl.pallas_call(
        functools.partial(kernel, n_hid, n_wid, n_dat),
        out_shape=(
            jax.ShapeDtypeStruct((own, width), bf16),
            jax.ShapeDtypeStruct((rank, hid), f32),
            jax.ShapeDtypeStruct((rank, hid), f32),
            jax.ShapeDtypeStruct((rank, width), f32),
        ),
        in_specs=[any_spec] * 5 + [smem_spec] * 3 + [any_spec] * 6,
        out_specs=(vmem_spec,) * 4,
        scratch_shapes=[
            V((3, cap + 1, step, step), bf16),
            V((8, lanes), jnp.int32),
            pltpu.SMEM((8, lanes), jnp.int32),
            V((width, 2 * hid), bf16),
            V((hid, width), bf16),
            V((2 * rank, 2 * hid), bf16),
            V((2, width, rank), bf16),
            V((width, 2 * rank), bf16),
            V((hid, rank), bf16),
            V((rank, width), bf16),
            V((n_hid, own, width), bf16),
            V((n_hid, own, width), bf16),
            V((rows, width), bf16),
            V((rows, width), bf16),
            V((n_wid, rows, 2 * hid), bf16),
            V((n_wid, rows, 2 * rank), f32),
            V((n_wid, rows, hid), bf16),
            V((n_hid, own, width), bf16),
            V((n_hid, own, width), bf16),
            V((n_hid, rows, rank), f32),
            V((n_dat, rank, 2 * hid), f32),
            V((n_dat, rank, width), f32),
            V((n_hid, own, width), f32),
            D((12,)),
            *sems(n_hid), *sems(n_hid), *sems(n_wid), *sems(n_wid), *sems(n_wid),
            *sems(n_hid), *sems(n_hid), *sems(n_dat), *sems(n_dat),
        ],
        compiler_params=pltpu.CompilerParams(
            collective_id=0, has_side_effects=True, vmem_limit_bytes=56 * 1024 * 1024
        ),
    )(
        tokens, output_gradient,
        gate_weight_blocks, up_weight_blocks, down_weight_blocks,
        gate_block_places, up_block_places, down_block_places,
        gate_adapter_first, gate_adapter_second,
        up_adapter_first, up_adapter_second,
        down_adapter_first, down_adapter_second,
    )


def solution(mesh):
    sizes = (mesh.shape["hid"], mesh.shape["wid"], mesh.shape["dat"])
    return jax.shard_map(
        functools.partial(shards, *sizes),
        mesh=mesh,
        in_specs=(
            P(("grp", "hid", "dat"), "wid"),
            P(("grp", "hid", "dat"), "wid"),
            P("hid", "wid", None, None, None),
            P("hid", "wid", None),
            P("hid", "wid", None, None, None),
            P("hid", "wid", None),
            P("hid", "wid", None, None, None),
            P("hid", "wid", None),
            P("wid", None),
            P(None, "hid"),
            P("wid", None),
            P(None, "hid"),
            P("hid", None),
            P(None, "wid"),
        ),
        out_specs=(
            P(("grp", "hid", "dat"), "wid"),
            P("grp", "hid"),
            P("grp", "hid"),
            P("grp", "wid"),
        ),
        check_vma=False,
    )
```

time: 166 us -> 35.9 us (0.22)
  waiting for transfers between devices: 53.5 us -> 0 us
  blocking collectives: 50.5 us -> 0 us
  matrix products: 24.5 us -> 0 us
  Pallas kernels: 0 us -> 24 us
  between operations: 14.1 us -> 0.64 us
  other arithmetic: 7.89 us -> 0 us
  local copies, waits for them, and re-layouts: 14 us -> 10.9 us
    psum x3 -> x0, waiting for transfers between devices: 48.7 us -> none  [the longest x2 39.8 us: shards(): lax.psum((gate_gradient_piece, up_gradient_piece, down_gradient_piece), '...]
    all_gather x2 -> x0, blocking collectives: 28.8 us -> none  [the longest x1 15.3 us: shards(): lax.all_gather(tokens, 'hid', axis=0, tiled=True)]
    dot_general x24 -> x0, matrix products: 24.5 us -> none  [the longest x9 7.49 us: wide_dot(): jnp.dot(left.astype(jnp.float32), right.astype(jnp.float32), precision=hi...]
    pallas_call x0 -> x1, Pallas kernels: none -> 24 us  [shards(): pl.pallas_call(functools.partial(kernel, n_hid, n_wid, n_dat), out_shape=...]
    psum x2 -> x0, blocking collectives: 21.8 us -> none  [the longest x1 12.2 us: shards(): down_rank_rows = lax.psum(down_rank_piece, 'hid')]
    gather x5 -> x0, local copies, waits for them, and re-layouts: 7.07 us -> none  [the longest x3 4.09 us: into_hidden(): picked = jnp.take(split_rows, slot_index % wid_blocks, axis=1)]
    reduce_scatter x1 -> x0, waiting for transfers between devices: 4.79 us -> none  [shards(): lax.psum_scatter(term_value + adapter_scale * rank_product, 'hid', scatte...]
    unnamed x58 -> x7, local copies, waits for them, and re-layouts: 6.18 us -> 10.9 us
  transfers between devices with their start and end apart: 4 -> 0, of which waited for: 4 -> 0; matrix products, arithmetic and copies ran while one was open for 6% -> 0% of each run, Pallas kernels for 0% -> 0%
where the time goes in v1:
time: 35.9 us; the launch traced here: 35.5 us
  Pallas kernels  24 us (67%)
  local copies, waits for them, and re-layouts  10.9 us (30%)
  between operations  0.64 us (2%)
    pallas_call x1, Pallas kernels, shards(): pl.pallas_call(functools.partial(kernel, n_hid, n_wid, n_dat), out_shape=...  24 us
    unnamed x7, local copies, waits for them, and re-layouts  10.9 us

profile of v1, /device:TPU:0, one launch (start us, length us, event | category | flops | bytes accessed | tf_op | source)
XLA Modules:
  0.0 35.5 jit_solution(1689998920695140587)
XLA Ops:
  0.6 1.5 %copy.20.ad = bf16[512,16]{1,0:T(8,128)(2,1)} copy(bf16[512,16]{0,1:T(8,128)(2,1)} %param.26) | data formatting | bytes 32768 | tf_op args[12]
  2.1 1.8 %copy.18.ag = bf16[2048,16]{1,0:T(8,128)(2,1)} copy(bf16[2048,16]{0,1:T(8,128)(2,1)} %param.22) | data formatting | bytes 131072 | tf_op args[8]
  3.9 1.9 %copy.19.au = bf16[2048,16]{1,0:T(8,128)(2,1)} copy(bf16[2048,16]{0,1:T(8,128)(2,1)} %param.24) | data formatting | bytes 131072 | tf_op args[10]
  5.8 24.0 %shard_map.165 = (bf16[8,2048]{1,0:T(8,128)(2,1)}, f32[16,512]{1,0:T(8,128)}, f32[16,512]{1,0:T(8,128)}, f32[16,2048]{1,0:T(8,128)}) custom-call(bf16[8,2048]{1,0:T(8,128)(2,1)} %tok.1, bf16[8,2048]{1,0:T(8,128)(2,1)} %dy.1, bf16[1,1,48,128,128]{4,3,2,1,0:T(8,128)(2,1)} %wg.1, bf16[1,1,48,128,128]{4,3,2,1,0:T(8,128)(2,1)} %wu.1, ...), custom_call_target="tpu_custom_call" | custom-call | tf_op jit(solution)/shard_map/pallas_call | solution.py:232
  29.8 1.4 %copy.25 = bf16[8,2048]{1,0:T(8,128)(2,1)} copy(bf16[8,2048]{1,0:T(8,128)(2,1)} %get-tuple-element.8) | data formatting | bytes 65536
  31.1 1.4 %copy.26 = f32[16,512]{1,0:T(8,128)} copy(f32[16,512]{1,0:T(8,128)} %get-tuple-element.9) | data formatting | bytes 65536
  32.5 1.4 %copy.27 = f32[16,512]{1,0:T(8,128)} copy(f32[16,512]{1,0:T(8,128)} %get-tuple-element.10) | data formatting | bytes 65536
  33.9 1.6 %copy.28 = f32[16,2048]{1,0:T(8,128)} copy(f32[16,2048]{1,0:T(8,128)} %get-tuple-element.11) | data formatting | bytes 262144

commit v2 on v1

--- a/solution.py
+++ b/solution.py
@@ -35,7 +35,7 @@
     n_hid, n_wid, n_dat,
     tok, dy, wg, wu, wd, pg, pu, pd, ag, bg, au, bu, ad, bd,
     tok_out, gate_out, up_out, down_out,
-    slots, inv_v, inv_s, wcat, wdn, bcat, a_first, a2, ad_v, bd_v,
+    slots, places, inv_v, inv_s, wcat, wdn, bcat, a2, ad_v, bd_v,
     xg, yg, x_v, y_v, fbuf, rbuf, hbuf, sbuf, tbuf, dbuf, gbuf, ebuf, acc,
     local_sem, x_s, x_r, y_s, y_r, f_s, f_r, r_s, r_r, h_s, h_r, t_s, t_r, d_s, d_r, g_s, g_r, e_s, e_r,
 ):
@@ -62,12 +62,15 @@
         (wg.at[0, 0], slots.at[0, pl.ds(0, cap)]),
         (wu.at[0, 0], slots.at[1, pl.ds(0, cap)]),
         (wd.at[0, 0], slots.at[2, pl.ds(0, cap)]),
-        (ag, a_first.at[0]),
-        (au, a_first.at[1]),
+        (ag, a2.at[pl.ds(0, rank)]),
+        (au, a2.at[pl.ds(rank, rank)]),
         (bg, bcat.at[pl.ds(0, rank), pl.ds(0, hid)]),
         (bu, bcat.at[pl.ds(rank, rank), pl.ds(hid, hid)]),
         (ad, ad_v),
         (bd, bd_v),
+        (pg.at[0], places.at[0]),
+        (pu.at[0], places.at[1]),
+        (pd.at[0], places.at[2]),
     ]
     local = [pltpu.make_async_copy(s, d, local_sem.at[i]) for i, (s, d) in enumerate(pairs)]
     for copy in local:
@@ -103,10 +106,11 @@
     lane = lax.broadcasted_iota(jnp.int32, (8, lanes), 1)
     row = lax.broadcasted_iota(jnp.int32, (8, lanes), 0)
     inverse = jnp.full((8, lanes), cap, jnp.int32)
-    for m, places in enumerate((pg, pu, pd)):
+    for m in range(3):
+        local[11 + m].wait()
         mine = jnp.where(row == m, lane, -1)
         for k in range(cap):
-            inverse = jnp.where(mine == places[0, 0, k], k, inverse)
+            inverse = jnp.where(mine == places[m, 0, k], k, inverse)
     inv_v[...] = inverse
     inv_copy = pltpu.make_async_copy(inv_v, inv_s, local_sem.at[len(pairs)])
     inv_copy.start()
@@ -114,10 +118,8 @@
         slots[m, cap] = jnp.zeros((step, step), bf16)
     bcat[:rank, hid:] = jnp.zeros((rank, hid), bf16)
     bcat[rank:, :hid] = jnp.zeros((rank, hid), bf16)
-    for copy in local[5:]:
+    for copy in local[5:11]:
         copy.wait()
-    a2[:, :rank] = a_first[0]
-    a2[:, rank:] = a_first[1]
     inv_copy.wait()
     for copy in local[2:5]:
         copy.wait()
@@ -141,10 +143,10 @@
     local[0].wait()
     arrive(xg, *hid_axis, x_s, x_r)
     assemble(xg, x_v)
-    ranks = dot(x_v[...], a2[...])
+    ranks = dot_nt(x_v[...], a2[...])
     rbuf[me_w] = ranks
     low_rank = wide(dot(two_parts(ranks), bcat[...]))
-    fbuf[me_w] = (dot(x_v[...], wcat[...]) + adapter_scale * low_rank).astype(bf16)
+    fbuf[me_w] = dot(x_v[...], wcat[...]) + adapter_scale * low_rank
     sent += send(lambda peer: fbuf.at[me_w], fbuf, *wid_axis, f_s, f_r)
     sent += send(lambda peer: rbuf.at[me_w], rbuf, *wid_axis, r_s, r_r)
 
@@ -152,19 +154,19 @@
     arrive(yg, *hid_axis, y_s, y_r)
     assemble(yg, y_v)
     grad_rank = dot_nt(y_v[...], bd_v[...])
-    back_low = wide(dot_nt(two_parts(grad_rank), ad_v[...]))
+    back_low = wide(dot(two_parts(grad_rank), ad_v[...]))
     hbuf[me_w] = (dot_nt(y_v[...], wdn[...]) + adapter_scale * back_low).astype(bf16)
     sent += send(lambda peer: hbuf.at[me_w], hbuf, *wid_axis, h_s, h_r)
 
     arrive(fbuf, *wid_axis, f_s, f_r)
     arrive(rbuf, *wid_axis, r_s, r_r)
-    both = sum(fbuf[i].astype(f32) for i in range(n_wid))
+    both = sum(fbuf[i] for i in range(n_wid))
     ranks = sum(rbuf[i] for i in range(n_wid))
     gate, up = both[:, :hid], both[:, hid:]
     sig = jax.nn.sigmoid(gate)
     act = gate * sig
     hidden = (act * up).astype(bf16)
-    dbuf[me_h] = dot(hidden, ad_v[...])
+    dbuf[me_h] = dot_nt(hidden, ad_v[...])
     sent += send(lambda peer: dbuf.at[me_h], dbuf, *hid_axis, d_s, d_r)
     slope = up * sig * (1.0 + gate * (1.0 - sig))
     arrive(hbuf, *wid_axis, h_s, h_r)
@@ -173,7 +175,7 @@
         [(hidden_grad * slope).astype(bf16), (hidden_grad * act).astype(bf16)], axis=1
     )
     backs = two_parts(adapter_scale * dot_nt(grads, bcat[...]))
-    total = dot_nt(grads, wcat[...]) + wide(dot_nt(backs, a2[...]))
+    total = dot_nt(grads, wcat[...]) + wide(dot(backs, a2[...]))
     for i in range(n_hid):
         sbuf[i] = total[i * own : (i + 1) * own].astype(bf16)
     acc[...] = total.reshape(n_hid, own, width)
@@ -202,6 +204,15 @@
     down_out[...] = sum(ebuf[i] for i in range(n_dat))
     for copy in sent:
         copy.wait_send()
+
+
+def hand_out(*refs):
+    sems = refs[8]
+    copies = [pltpu.make_async_copy(refs[i], refs[i + 4], sems.at[i]) for i in range(4)]
+    for copy in copies:
+        copy.start()
+    for copy in copies:
+        copy.wait()
 
 
 def shards(
@@ -221,40 +232,41 @@
     positions = (hid // step) * (width // step)
     lanes = -(-positions // 128) * 128
     any_spec = pl.BlockSpec(memory_space=pl.ANY)
-    smem_spec = pl.BlockSpec(memory_space=pltpu.SMEM)
     vmem_spec = pl.BlockSpec(memory_space=pltpu.VMEM)
     V = pltpu.VMEM
     D = pltpu.SemaphoreType.DMA
 
+    shapes = (
+        jax.ShapeDtypeStruct((own, width), bf16),
+        jax.ShapeDtypeStruct((rank, hid), f32),
+        jax.ShapeDtypeStruct((rank, hid), f32),
+        jax.ShapeDtypeStruct((rank, width), f32),
+    )
+
     def sems(n):
         return [D((max(n - 1, 1),)), D((n,))]
 
-    return pl.pallas_call(
+    results = pl.pallas_call(
         functools.partial(kernel, n_hid, n_wid, n_dat),
-        out_shape=(
-            jax.ShapeDtypeStruct((own, width), bf16),
-            jax.ShapeDtypeStruct((rank, hid), f32),
-            jax.ShapeDtypeStruct((rank, hid), f32),
-            jax.ShapeDtypeStruct((rank, width), f32),
-        ),
-        in_specs=[any_spec] * 5 + [smem_spec] * 3 + [any_spec] * 6,
+        out_shape=shapes,
+        in_specs=[any_spec] * 14,
         out_specs=(vmem_spec,) * 4,
         scratch_shapes=[
             V((3, cap + 1, step, step), bf16),
+            pltpu.SMEM((3, 1, cap), jnp.int32),
             V((8, lanes), jnp.int32),
             pltpu.SMEM((8, lanes), jnp.int32),
             V((width, 2 * hid), bf16),
             V((hid, width), bf16),
             V((2 * rank, 2 * hid), bf16),
-            V((2, width, rank), bf16),
-            V((width, 2 * rank), bf16),
-            V((hid, rank), bf16),
+            V((2 * rank, width), bf16),
+            V((rank, hid), bf16),
             V((rank, width), bf16),
             V((n_hid, own, width), bf16),
             V((n_hid, own, width), bf16),
             V((rows, width), bf16),
             V((rows, width), bf16),
-            V((n_wid, rows, 2 * hid), bf16),
+            V((n_wid, rows, 2 * hid), f32),
             V((n_wid, rows, 2 * rank), f32),
             V((n_wid, rows, hid), bf16),
             V((n_hid, own, width), bf16),
@@ -263,21 +275,33 @@
             V((n_dat, rank, 2 * hid), f32),
             V((n_dat, rank, width), f32),
             V((n_hid, own, width), f32),
-            D((12,)),
+            D((15,)),
             *sems(n_hid), *sems(n_hid), *sems(n_wid), *sems(n_wid), *sems(n_wid),
             *sems(n_hid), *sems(n_hid), *sems(n_dat), *sems(n_dat),
         ],
         compiler_params=pltpu.CompilerParams(
-            collective_id=0, has_side_effects=True, vmem_limit_bytes=56 * 1024 * 1024
+            collective_id=0, has_side_effects=True, vmem_limit_bytes=40 * 1024 * 1024
         ),
     )(
-        tokens, output_gradient,
-        gate_weight_blocks, up_weight_blocks, down_weight_blocks,
-        gate_block_places, up_block_places, down_block_places,
-        gate_adapter_first, gate_adapter_second,
-        up_adapter_first, up_adapter_second,
-        down_adapter_first, down_adapter_second,
+        *(
+            pltpu.with_memory_space_constraint(operand, pltpu.HBM)
+            for operand in (
+                tokens, output_gradient,
+                gate_weight_blocks, up_weight_blocks, down_weight_blocks,
+                gate_block_places, up_block_places, down_block_places,
+                gate_adapter_first.T, gate_adapter_second,
+                up_adapter_first.T, up_adapter_second,
+                down_adapter_first.T, down_adapter_second,
+            )
+        ),
     )
+    return pl.pallas_call(
+        hand_out,
+        out_shape=shapes,
+        in_specs=[any_spec] * 4,
+        out_specs=(any_spec,) * 4,
+        scratch_shapes=[D((4,))],
+    )(*results)
 
 
 def solution(mesh):

time: 35.9 us -> 34.4 us (0.958)
  local copies, waits for them, and re-layouts: 10.9 us -> 2.47 us
  Pallas kernels: 24 us -> 31.2 us
    unnamed x7 -> x8, local copies, waits for them, and re-layouts: 10.9 us -> 2.47 us
    pallas_call x0 -> x1, Pallas kernels: none -> 8.08 us  [shards(): pl.pallas_call(hand_out, out_shape=shapes, in_specs=[any_spec] * 4, out_s...]
    pallas_call x1, Pallas kernels: 24 us -> 23.1 us  [shards(): pl.pallas_call(functools.partial(kernel, n_hid, n_wid, n_dat), out_shape=...]
where the time goes in v2:
time: 34.4 us; the launch traced here: 34.3 us
  Pallas kernels  31.2 us (91%)
  local copies, waits for them, and re-layouts  2.47 us (7%)
  between operations  0.66 us (2%)
    pallas_call x1, Pallas kernels, shards(): pl.pallas_call(functools.partial(kernel, n_hid, n_wid, n_dat), out_shape=...  23.1 us
    pallas_call x1, Pallas kernels, shards(): pl.pallas_call(hand_out, out_shape=shapes, in_specs=[any_spec] * 4, out_s...  8.08 us
    unnamed x8, local copies, waits for them, and re-layouts  2.47 us

profile of v2, /device:TPU:0, one launch (start us, length us, event | category | flops | bytes accessed | tf_op | source)
XLA Modules:
  0.0 34.3 jit_solution(8743852939538180229)
XLA Ops:
  0.6 23.1 %shard_map.165 = (bf16[8,2048]{1,0:T(8,128)(2,1)S(1)}, f32[16,512]{1,0:T(8,128)S(1)}, f32[16,512]{1,0:T(8,128)S(1)}, f32[16,2048]{1,0:T(8,128)S(1)}) custom-call(bf16[8,2048]{1,0:T(8,128)(2,1)} %tok.1, bf16[8,2048]{1,0:T(8,128)(2,1)} %dy.1, bf16[1,1,48,128,128]{4,3,2,1,0:T(8,128)(2,1)} %wg.1, bf16[1,1,48,128,128]{4,3,2,1,0:T(8,128)(2,1)} %wu.1, ...), custom_call_target="tpu_custom_call" | custom-call | tf_op jit(solution)/shard_map/pallas_call | solution.py:249
  23.7 0.0 copy-start
  23.7 0.6 %copy-done = f32[16,2048]{1,0:T(8,128)} copy-done((f32[16,2048]{1,0:T(8,128)}, f32[16,2048]{1,0:T(8,128)S(1)}, u32[]{:S(2)}) %copy-start) | copy-done | bytes 131096
  24.4 0.0 copy-start.1
  24.4 0.6 %copy-done.1 = bf16[8,2048]{1,0:T(8,128)(2,1)} copy-done((bf16[8,2048]{1,0:T(8,128)(2,1)}, bf16[8,2048]{1,0:T(8,128)(2,1)S(1)}, u32[]{:S(2)}) %copy-start.1) | copy-done | bytes 32792
  25.0 0.0 copy-start.2
  25.0 0.6 %copy-done.2 = f32[16,512]{1,0:T(8,128)} copy-done((f32[16,512]{1,0:T(8,128)}, f32[16,512]{1,0:T(8,128)S(1)}, u32[]{:S(2)}) %copy-start.2) | copy-done | bytes 32792
  25.6 0.0 copy-start.3
  25.6 0.6 %copy-done.3 = f32[16,512]{1,0:T(8,128)} copy-done((f32[16,512]{1,0:T(8,128)}, f32[16,512]{1,0:T(8,128)S(1)}, u32[]{:S(2)}) %copy-start.3) | copy-done | bytes 32792
  26.2 8.1 %shard_map.166 = (bf16[8,2048]{1,0:T(8,128)(2,1)}, f32[16,512]{1,0:T(8,128)}, f32[16,512]{1,0:T(8,128)}, f32[16,2048]{1,0:T(8,128)}) custom-call(bf16[8,2048]{1,0:T(8,128)(2,1)} %copy-done.1, f32[16,512]{1,0:T(8,128)} %copy-done.2, f32[16,512]{1,0:T(8,128)} %copy-done.3, f32[16,2048]{1,0:T(8,128)} %copy-done), custom_call_target="tpu_custom_call" | custom-call | tf_op jit(solution)/shard_map/pallas_call | solution.py:298
Async XLA Ops:
  23.7 0.7 %copy-start = (f32[16,2048]{1,0:T(8,128)}, f32[16,2048]{1,0:T(8,128)S(1)}, u32[]{:S(2)}) copy-start(f32[16,2048]{1,0:T(8,128)S(1)} %get-tuple-element.11.refs_3_) | copy-start | bytes 393220
  24.4 0.6 %copy-start.1 = (bf16[8,2048]{1,0:T(8,128)(2,1)}, bf16[8,2048]{1,0:T(8,128)(2,1)S(1)}, u32[]{:S(2)}) copy-start(bf16[8,2048]{1,0:T(8,128)(2,1)S(1)} %get-tuple-element.8.refs_0_) | copy-start | bytes 98308
  25.0 0.6 %copy-start.2 = (f32[16,512]{1,0:T(8,128)}, f32[16,512]{1,0:T(8,128)S(1)}, u32[]{:S(2)}) copy-start(f32[16,512]{1,0:T(8,128)S(1)} %get-tuple-element.9.refs_1_) | copy-start | bytes 98308
  25.6 0.6 %copy-start.3 = (f32[16,512]{1,0:T(8,128)}, f32[16,512]{1,0:T(8,128)S(1)}, u32[]{:S(2)}) copy-start(f32[16,512]{1,0:T(8,128)S(1)} %get-tuple-element.10.refs_2_) | copy-start | bytes 98308

commit v3 on v2

--- a/solution.py
+++ b/solution.py
@@ -298,10 +298,10 @@
     return pl.pallas_call(
         hand_out,
         out_shape=shapes,
-        in_specs=[any_spec] * 4,
+        in_specs=[vmem_spec] * 4,
         out_specs=(any_spec,) * 4,
         scratch_shapes=[D((4,))],
-    )(*results)
+    )(*(pltpu.with_memory_space_constraint(result, pltpu.VMEM) for result in results))
 
 
 def solution(mesh):

time: 34.4 us -> 24.6 us (0.72)
  Pallas kernels: 31.2 us -> 23.8 us
  local copies, waits for them, and re-layouts: 2.47 us -> 0 us
    pallas_call x1, Pallas kernels: 8.08 us -> 0.73 us  [shards(): pl.pallas_call(hand_out, out_shape=shapes, in_specs=[vmem_spec] * 4, out_...]
    unnamed x8 -> x0, local copies, waits for them, and re-layouts: 2.47 us -> none
where the time goes in v3:
time: 24.6 us; the launch traced here: 24.4 us
  Pallas kernels  23.8 us (97%)
  between operations  0.64 us (3%)
    pallas_call x1, Pallas kernels, shards(): pl.pallas_call(functools.partial(kernel, n_hid, n_wid, n_dat), out_shape=...  23.1 us
    pallas_call x1, Pallas kernels, shards(): pl.pallas_call(hand_out, out_shape=shapes, in_specs=[vmem_spec] * 4, out_...  0.73 us

profile of v3, /device:TPU:0, one launch (start us, length us, event | category | flops | bytes accessed | tf_op | source)
XLA Modules:
  0.0 24.4 jit_solution(2956180660277335207)
XLA Ops:
  0.6 23.1 %shard_map.165 = (bf16[8,2048]{1,0:T(8,128)(2,1)S(1)}, f32[16,512]{1,0:T(8,128)S(1)}, f32[16,512]{1,0:T(8,128)S(1)}, f32[16,2048]{1,0:T(8,128)S(1)}) custom-call(bf16[8,2048]{1,0:T(8,128)(2,1)} %tok.1, bf16[8,2048]{1,0:T(8,128)(2,1)} %dy.1, bf16[1,1,48,128,128]{4,3,2,1,0:T(8,128)(2,1)} %wg.1, bf16[1,1,48,128,128]{4,3,2,1,0:T(8,128)(2,1)} %wu.1, ...), custom_call_target="tpu_custom_call" | custom-call | tf_op jit(solution)/shard_map/pallas_call | solution.py:249
  23.7 0.7 %shard_map.166 = (bf16[8,2048]{1,0:T(8,128)(2,1)}, f32[16,512]{1,0:T(8,128)}, f32[16,512]{1,0:T(8,128)}, f32[16,2048]{1,0:T(8,128)}) custom-call(bf16[8,2048]{1,0:T(8,128)(2,1)S(1)} %get-tuple-element.8.refs_0_, f32[16,512]{1,0:T(8,128)S(1)} %get-tuple-element.9.refs_1_, f32[16,512]{1,0:T(8,128)S(1)} %get-tuple-element.10.refs_2_, ...), custom_call_target="tpu_custom_call" | custom-call | tf_op jit(solution)/shard_map/pallas_call | solution.py:298

commit v4 on v3

--- a/solution.py
+++ b/solution.py
@@ -35,7 +35,7 @@
     n_hid, n_wid, n_dat,
     tok, dy, wg, wu, wd, pg, pu, pd, ag, bg, au, bu, ad, bd,
     tok_out, gate_out, up_out, down_out,
-    slots, places, inv_v, inv_s, wcat, wdn, bcat, a2, ad_v, bd_v,
+    slots, places, inv_v, inv_s, wback, wcat, wdn, bcat, a2, ad_v, bd_v,
     xg, yg, x_v, y_v, fbuf, rbuf, hbuf, sbuf, tbuf, dbuf, gbuf, ebuf, acc,
     local_sem, x_s, x_r, y_s, y_r, f_s, f_r, r_s, r_r, h_s, h_r, t_s, t_r, d_s, d_r, g_s, g_r, e_s, e_r,
 ):
@@ -131,10 +131,21 @@
                 wcat[pl.ds(start, step), m * hid + h * step : m * hid + (h + 1) * step] = slots[
                     m, inv_s[m, h * wb + w]
                 ]
-            wdn[h * step : (h + 1) * step, pl.ds(start, step)] = slots[2, inv_s[2, h * wb + w]]
+            wdn[pl.ds(start, step), h * step : (h + 1) * step] = slots[2, inv_s[2, h * wb + w]].T
         return carry
 
     lax.fori_loop(0, wb, lay, 0)
+
+    def lay_back(w, carry):
+        start = pl.multiple_of(w * step, step)
+        for h in range(hb):
+            for m in (0,):
+                wback[m * hid + h * step : m * hid + (h + 1) * step, pl.ds(start, step)] = wcat[
+                    pl.ds(start, step), m * hid + h * step : m * hid + (h + 1) * step
+                ].T
+        return carry
+
+    lax.fori_loop(0, wb, lay_back, 0)
 
     def assemble(gathered, whole):
         parts = [gathered[i].astype(f32) for i in range(n_hid)]
@@ -155,8 +166,19 @@
     assemble(yg, y_v)
     grad_rank = dot_nt(y_v[...], bd_v[...])
     back_low = wide(dot(two_parts(grad_rank), ad_v[...]))
-    hbuf[me_w] = (dot_nt(y_v[...], wdn[...]) + adapter_scale * back_low).astype(bf16)
+    hbuf[me_w] = (dot(y_v[...], wdn[...]) + adapter_scale * back_low).astype(bf16)
     sent += send(lambda peer: hbuf.at[me_w], hbuf, *wid_axis, h_s, h_r)
+
+    def lay_back_up(w, carry):
+        start = pl.multiple_of(w * step, step)
+        for h in range(hb):
+            for m in (1,):
+                wback[m * hid + h * step : m * hid + (h + 1) * step, pl.ds(start, step)] = wcat[
+                    pl.ds(start, step), m * hid + h * step : m * hid + (h + 1) * step
+                ].T
+        return carry
+
+    lax.fori_loop(0, wb, lay_back_up, 0)
 
     arrive(fbuf, *wid_axis, f_s, f_r)
     arrive(rbuf, *wid_axis, r_s, r_r)
@@ -175,7 +197,7 @@
         [(hidden_grad * slope).astype(bf16), (hidden_grad * act).astype(bf16)], axis=1
     )
     backs = two_parts(adapter_scale * dot_nt(grads, bcat[...]))
-    total = dot_nt(grads, wcat[...]) + wide(dot(backs, a2[...]))
+    total = dot(grads, wback[...]) + wide(dot(backs, a2[...]))
     for i in range(n_hid):
         sbuf[i] = total[i * own : (i + 1) * own].astype(bf16)
     acc[...] = total.reshape(n_hid, own, width)
@@ -256,8 +278,9 @@
             pltpu.SMEM((3, 1, cap), jnp.int32),
             V((8, lanes), jnp.int32),
             pltpu.SMEM((8, lanes), jnp.int32),
+            V((2 * hid, width), bf16),
             V((width, 2 * hid), bf16),
-            V((hid, width), bf16),
+            V((width, hid), bf16),
             V((2 * rank, 2 * hid), bf16),
             V((2 * rank, width), bf16),
             V((rank, hid), bf16),

time: 24.6 us -> 24 us (0.976)
  Pallas kernels: 23.8 us -> 23.3 us
    pallas_call x1, Pallas kernels: 23.1 us -> 22.5 us  [shards(): pl.pallas_call(functools.partial(kernel, n_hid, n_wid, n_dat), out_shape=...]
where the time goes in v4:
time: 24 us; the launch traced here: 23.9 us
  Pallas kernels  23.3 us (97%)
  between operations  0.64 us (3%)
    pallas_call x1, Pallas kernels, shards(): pl.pallas_call(functools.partial(kernel, n_hid, n_wid, n_dat), out_shape=...  22.5 us
    pallas_call x1, Pallas kernels, shards(): pl.pallas_call(hand_out, out_shape=shapes, in_specs=[vmem_spec] * 4, out_...  0.73 us

profile of v4, /device:TPU:0, one launch (start us, length us, event | category | flops | bytes accessed | tf_op | source)
XLA Modules:
  0.0 23.9 jit_solution(10455800625638012165)
XLA Ops:
  0.6 22.5 %shard_map.165 = (bf16[8,2048]{1,0:T(8,128)(2,1)S(1)}, f32[16,512]{1,0:T(8,128)S(1)}, f32[16,512]{1,0:T(8,128)S(1)}, f32[16,2048]{1,0:T(8,128)S(1)}) custom-call(bf16[8,2048]{1,0:T(8,128)(2,1)} %tok.1, bf16[8,2048]{1,0:T(8,128)(2,1)} %dy.1, bf16[1,1,48,128,128]{4,3,2,1,0:T(8,128)(2,1)} %wg.1, bf16[1,1,48,128,128]{4,3,2,1,0:T(8,128)(2,1)} %wu.1, ...), custom_call_target="tpu_custom_call" | custom-call | tf_op jit(solution)/shard_map/pallas_call | solution.py:271
  23.2 0.7 %shard_map.166 = (bf16[8,2048]{1,0:T(8,128)(2,1)}, f32[16,512]{1,0:T(8,128)}, f32[16,512]{1,0:T(8,128)}, f32[16,2048]{1,0:T(8,128)}) custom-call(bf16[8,2048]{1,0:T(8,128)(2,1)S(1)} %get-tuple-element.8.refs_0_, f32[16,512]{1,0:T(8,128)S(1)} %get-tuple-element.9.refs_1_, f32[16,512]{1,0:T(8,128)S(1)} %get-tuple-element.10.refs_2_, ...), custom_call_target="tpu_custom_call" | custom-call | tf_op jit(solution)/shard_map/pallas_call | solution.py:321
